TPU v7x, 32 devices: a whole 2x2x4 slice. The times are simulated.
32 devices in a mesh: dp: 4 (over y, x), mp: 8 (over z, core).
Axes of the slice: x: 2, y: 2, z: 4, core: 2. Of those that a mesh axis runs over, the one named last changes fastest.
Arguments:
- activations: bfloat16 [4096, 2048], P('dp', 'mp'), may hold values from -6 to 6
- out_grad: bfloat16 [4096, 8192], P('dp'), may hold values from -0.8984375 to 0.8984375
- old_weight: bfloat16 [8, 256, 8192], P('mp', 'dp'), may hold values from -0.125 to 0.125
- old_first: float32 [8, 256, 8192], P('mp', 'dp'), may hold values from -6 to 6
- old_second: float32 [8, 256, 8192], P('mp', 'dp'), may hold values from 0.25 to 4
- step: int32 [1], replicated, may hold values from 1 to 31
- next_input: bfloat16 [4096, 2048], P('dp', 'mp'), may hold values from -6 to 6
Outputs:
- new_weight: bfloat16 [8, 344, 8192], P('mp', 'dp')
- new_first: float32 [8, 344, 8192], P('mp', 'dp')
- new_second: float32 [8, 344, 8192], P('mp', 'dp')
- output: bfloat16 [4096, 8192], P('dp', 'mp')
Inputs may be any that keep to these rules, and one draw needn't show every extreme that they name: `step`: the number of Adam steps taken, this one included.
All inputs are finite; a program needn't handle non-finite values.
Results may differ from a plain program's by a relative error of at most 0.0049.
Values may be sent and summed in bfloat16 or wider, within the bound.
A program may use at most 192 MiB of HBM per device.

v0:
```python
import jax
import jax.numpy as jnp
from jax import lax
from jax.sharding import PartitionSpec as P


def partner(i, k, n):
    return i ^ k if n & n - 1 == 0 else (i + k) % n


def exchange(block, axis, k):
    n = lax.axis_size(axis)
    return lax.ppermute(block, axis, [(i, partner(i, k, n)) for i in range(n)])


def target(k, n, axis):
    me = lax.axis_index(axis)
    return me ^ k if n & n - 1 == 0 else lax.rem(me + k, n)


def to_front(block, axis):
    n = lax.axis_size(axis)
    return lax.ppermute(block, axis, [(i, i - 1) for i in range(1, n)])


def body(activations, out_grad, old_weight, old_first, old_second, step, next_input):
    owners = lax.axis_size("dp")
    owner = lax.axis_index("dp")
    old_rows = old_weight.shape[1]
    width = old_weight.shape[2]
    held_rows = old_rows * owners
    shard_rows = (held_rows + owners - 2) // (owners - 1)
    input_all = lax.all_gather(next_input, "mp", axis=1, tiled=True)
    part = lax.dot_general(
        activations, out_grad, (((0,), (0,)), ((), ())), preferred_element_type=jnp.float32
    ).astype(jnp.bfloat16)
    part = part.reshape(owners, old_rows, width)
    grad = lax.dynamic_index_in_dim(part, owner, 0, keepdims=False).astype(jnp.float32)
    for k in range(1, owners):
        away = lax.dynamic_index_in_dim(part, target(k, owners, "dp"), 0, keepdims=False)
        grad = grad + exchange(away, "dp", k).astype(jnp.float32)
    step_float = step[0].astype(jnp.float32)
    first_fix = 1.0 - jnp.power(jnp.float32(0.9), step_float)
    second_fix = 1.0 - jnp.power(jnp.float32(0.95), step_float)
    new_first = 0.9 * old_first[0] + 0.1 * grad
    new_second = 0.95 * old_second[0] + 0.05 * grad * grad
    update = new_first / first_fix / (jnp.sqrt(new_second / second_fix) + 1e-08)
    new_weight = (old_weight[0].astype(jnp.float32) - 0.01 * update).astype(jnp.bfloat16)
    weight_part = lax.all_to_all(new_weight, "mp", split_axis=1, concat_axis=0, tiled=True)
    heads = lax.axis_size("mp")
    weight_part = weight_part.reshape(heads, old_rows, -1)
    weight_cols = lax.all_gather(weight_part, "dp", axis=1, tiled=True)
    weight_cols = weight_cols.reshape(heads * held_rows, -1)
    begin = owner * (shard_rows - old_rows)

    def mine(block):
        behind = to_front(block.astype(jnp.bfloat16), "dp").astype(block.dtype)
        rows = jnp.concatenate([block, behind, jnp.zeros((shard_rows, width), block.dtype)], 0)
        return lax.dynamic_slice_in_dim(rows, begin, shard_rows, 0)[None]

    outs = (mine(new_weight), mine(new_first), mine(new_second))
    output = jnp.dot(input_all, weight_cols, preferred_element_type=jnp.float32).astype(
        jnp.bfloat16
    )
    return (*outs, output)


def solution(mesh):
    return jax.shard_map(
        body,
        mesh=mesh,
        in_specs=(
            P("dp", "mp"),
            P("dp", None),
            P("mp", "dp", None),
            P("mp", "dp", None),
            P("mp", "dp", None),
            P(),
            P("dp", "mp"),
        ),
        out_specs=(P("mp", "dp", None), P("mp", "dp", None), P("mp", "dp", None), P("dp", "mp")),
        check_vma=False,
    )
```

profile of v0, /device:TPU:0, one launch (start us, length us, event | category | flops | bytes accessed | tf_op | source)
XLA Modules:
  0.0 292.9 jit_solution(17170010049314651664)
XLA Ops:
  7.2 0.0 copy-start
  7.2 0.0 all-gather.3.cloned.1.call-start
  7.2 1.0 copy-done
  8.2 10.7 %convolution_convert_fusion = bf16[256,8192]{1,0:T(8,128)(2,1)S(1)} fusion(bf16[1024,256]{1,0:T(8,128)(2,1)S(1)} %copy-done, bf16[1024,8192]{1,0:T(8,128)(2,1)} %param.8), kind=kOutput, calls=%fused_computation | convolution fusion | flops 4297064448 | bytes 21495808 | tf_op jit(solution)/shard_map/dot_general | solution.py:34
  19.0 0.0 copy-start.4
  19.0 1.8 dynamic-slice_bitcast_fusion.2
  20.7 1.2 copy-done.4
  21.9 2.9 %collective-permute-start = (bf16[64,8192]{1,0:T(8,128)(2,1)}, bf16[64,8192]{1,0:T(8,128)(2,1)S(1)}, u32[]{:S(2)}, u32[]{:S(2)}) collective-permute-start(bf16[64,8192]{1,0:T(8,128)(2,1)} %get-tuple-element.26), channel_id=1, source_target_pairs={{0,8},{8,0},{16,24},{24,16},{1,9},{9,1},{17,25},{25,17},{2,10},{10... | collective-permute-start | bytes 3145736 | tf_op jit(solution)/shard_map/ppermute | solution.py:13
  24.8 1.5 collective-permute-start.1
  26.4 0.0 collective-permute-start.2
  27.1 0.0 copy-start.9
  27.1 21.9 %collective-permute-done = bf16[64,8192]{1,0:T(8,128)(2,1)S(1)} collective-permute-done((bf16[64,8192]{1,0:T(8,128)(2,1)}, bf16[64,8192]{1,0:T(8,128)(2,1)S(1)}, u32[]{:S(2)}, u32[]{:S(2)}) %collective-permute-start) | collective-permute-done | bytes 1048608 | tf_op jit(solution)/shard_map/ppermute | solution.py:13
  49.0 23.1 %collective-permute-done.1 = bf16[64,8192]{1,0:T(8,128)(2,1)S(1)} collective-permute-done((bf16[64,8192]{1,0:T(8,128)(2,1)}, bf16[64,8192]{1,0:T(8,128)(2,1)S(1)}, u32[]{:S(2)}, u32[]{:S(2)}) %collective-permute-start.1) | collective-permute-done | bytes 1048608 | tf_op jit(solution)/shard_map/ppermute | solution.py:13
  72.1 0.0 copy-done.7
  72.2 1.0 copy-done.8
  73.1 0.0 collective-permute-done.2
  73.1 5.9 %fusion.11 = (bf16[64,8192]{1,0:T(8,128)(2,1)}, f32[64,8192]{1,0:T(8,128)S(1)}, bf16[64,8192]{1,0:T(8,128)(2,1)}, f32[64,8192]{1,0:T(8,128)S(1)}) fusion(bf16[64,8192]{1,0:T(8,128)(2,1)} %collective-permute-done.2, bf16[64,8192]{1,0:T(8,128)(2,1)} %copy-done.8, bf16[64,8192]{1,0:T(8,128)(2,1)} %copy-done.7, bf16[4,64,8192]{2,1,0:T(8,128)(2,1)} %bitcast.42, ...), kind=kLoop, calls=%fused_computation.29 | loop fusion | flops 8388608 | bytes 14680068 | tf_op jit(solution)/shard_map/convert_element_type | solution.py:57
  79.0 0.0 copy-done.9
  79.0 1.1 fusion.7
  80.1 0.2 copy-done.2
  80.3 0.1 copy.21
  80.4 31.3 %all_to_all.16 = bf16[64,8,1024]{2,0,1:T(8,128)(2,1)S(1)} all-to-all(bf16[64,8,1024]{2,0,1:T(8,128)(2,1)S(1)} %bitcast.46), channel_id=1, replica_groups=mesh['dp'=4,'mp'=8] {'mp'}, dimensions={1} | all-to-all | bytes 2097152 | tf_op jit(solution)/shard_map/all_to_all | solution.py:49
  111.7 1.5 copy.16
  113.2 0.0 all-gather.3.cloned.1.call-update
  113.2 0.0 all-gather.5.cloned.1.call-start
  113.3 0.7 all-gather.5.cloned.1.call-update
  114.0 1.3 collective-permute-start.4
  115.3 1.3 collective-permute-start.5
  116.6 0.1 pad_dynamic-slice_fusion.6
  116.7 0.1 pad_dynamic-slice_fusion.7
  116.8 1.5 collective-permute-start.3
  118.2 35.3 %collective-permute-done.4 = bf16[64,8192]{1,0:T(8,128)(2,1)} collective-permute-done((bf16[64,8192]{1,0:T(8,128)(2,1)}, bf16[64,8192]{1,0:T(8,128)(2,1)}, u32[]{:S(2)}, u32[]{:S(2)}) %collective-permute-start.4) | collective-permute-done | bytes 1048608 | tf_op jit(solution)/shard_map/ppermute | solution.py:23
  153.5 1.4 convert_element_type.60
  154.9 0.0 copy-start.3
  154.9 21.1 %collective-permute-done.5 = bf16[64,8192]{1,0:T(8,128)(2,1)} collective-permute-done((bf16[64,8192]{1,0:T(8,128)(2,1)}, bf16[64,8192]{1,0:T(8,128)(2,1)}, u32[]{:S(2)}, u32[]{:S(2)}) %collective-permute-start.5) | collective-permute-done | bytes 1048608 | tf_op jit(solution)/shard_map/ppermute | solution.py:23
  176.0 1.4 convert_element_type.62
  177.4 0.0 copy-done.3
  177.4 4.0 %fusion.1 = (f32[86,8192]{1,0:T(8,128)}, f32[86,8192]{1,0:T(8,128)}) fusion(s32[]{:T(128)S(6)} %select_n.22, f32[64,8192]{1,0:T(8,128)S(1)} %get-tuple-element.21, f32[64,8192]{1,0:T(8,128)S(1)} %convert_element_type.62, f32[86]{0:T(128)S(1)} %pad_dynamic-slice_fusion.6, f32[64,8192]{1,0:T(8,128)S(1)} %convert_element_type.60, f32[64,8192]{1,0:T(8,128)S(1)} %copy-done.3), kind=kLoop, calls=%fused_computation.9 | loop fusion | flops 2818048 | bytes 14025052 | tf_op jit(solution)/shard_map/concatenate | solution.py:58
  181.3 6.7 %broadcast_in_dim.14 = f32[1,86,8192]{2,0,1:T(1,128)} reshape(f32[86,8192]{1,0:T(8,128)} %get-tuple-element.30) | data formatting | bytes 5636096 | tf_op jit(solution)/shard_map/broadcast_in_dim | solution.py:59
  188.0 0.0 copy-done.5
  188.0 4.7 %broadcast_in_dim.15 = f32[1,86,8192]{2,0,1:T(1,128)} reshape(f32[86,8192]{1,0:T(8,128)S(1)} %copy-done.5) | data formatting | bytes 5636096 | tf_op jit(solution)/shard_map/broadcast_in_dim | solution.py:59
  192.8 4.1 %collective-permute-done.3 = bf16[64,8192]{1,0:T(8,128)(2,1)} collective-permute-done((bf16[64,8192]{1,0:T(8,128)(2,1)}, bf16[64,8192]{1,0:T(8,128)(2,1)}, u32[]{:S(2)}, u32[]{:S(2)}) %collective-permute-start.3) | collective-permute-done | bytes 1048608 | tf_op jit(solution)/shard_map/ppermute | solution.py:23
  196.9 3.4 %fusion.10 = bf16[1,86,8192]{2,1,0:T(8,128)(2,1)} fusion(s32[]{:T(128)S(6)} %select_n.22, bf16[64,8192]{1,0:T(8,128)(2,1)} %copy-done.6, bf16[64,8192]{1,0:T(8,128)(2,1)} %collective-permute-done.3, bf16[86]{0:T(256)(128)(2,1)S(1)} %pad_dynamic-slice_fusion.7), kind=kLoop, calls=%fused_computation.22 | loop fusion | flops 4227072 | bytes 3506352 | tf_op jit(solution)/shard_map/broadcast_in_dim | solution.py:59
  200.3 25.5 %all-gather.3.cloned.1.call-done = bf16[8,256,1024]{2,0,1:T(8,128)(2,1)} async-done(((bf16[8,64,1024]{2,0,1:T(8,128)(2,1)}), bf16[8,256,1024]{2,0,1:T(8,128)(2,1)}) %all-gather.3.cloned.1.call-update) | async-done | bytes 4194320 | tf_op jit(solution)/shard_map/all_gather | solution.py:52
  225.8 6.5 %copy.17 = bf16[8,256,1024]{2,1,0:T(8,128)(2,1)} copy(bf16[8,256,1024]{2,0,1:T(8,128)(2,1)} %all-gather.3.cloned.1.call-done) | data formatting | bytes 8388608 | tf_op jit(solution)/shard_map/all_gather | solution.py:52
  232.3 42.9 %all-gather.5.cloned.1.call-done = bf16[1024,2048]{1,0:T(8,128)(2,1)} async-done(((bf16[1024,256]{1,0:T(8,128)(2,1)}), bf16[1024,2048]{1,0:T(8,128)(2,1)}) %all-gather.5.cloned.1.call-update) | async-done | bytes 4194320 | tf_op jit(solution)/shard_map/all_gather | solution.py:33
  275.2 8.3 %convert_bitcast_fusion = bf16[1024,1024]{0,1:T(8,128)(2,1)S(1)} fusion(bf16[2048,1024]{1,0:T(8,128)(2,1)} %bitcast.44, bf16[1024,2048]{1,0:T(8,128)(2,1)} %all-gather.5.cloned.1.call-done), kind=kOutput, calls=%fused_computation.19 | convolution fusion | flops 4296015872 | bytes 10485760 | tf_op jit(solution)/shard_map/dot_general | solution.py:62
  283.5 2.6 copy.18
  (10 shorter events, 0.0 us)
Async XLA Ops:
  7.2 1.1 copy-start
  7.2 218.6 %all-gather.3.cloned.1.call-start = ((), (), s32[]{:S(2)}) async-start(), calls=%async_computation.1 | async-start | bytes 5242880 | tf_op jit(solution)/shard_map/all_gather | solution.py:52
  19.0 2.9 %copy-start.4 = (bf16[256,8192]{1,0:T(8,128)(2,1)}, bf16[256,8192]{1,0:T(8,128)(2,1)S(1)}, u32[]{:S(2)}) copy-start(bf16[256,8192]{1,0:T(8,128)(2,1)S(1)} %convolution_convert_fusion) | copy-start | bytes 12582916
  21.9 27.1 %collective-permute-start = (bf16[64,8192]{1,0:T(8,128)(2,1)}, bf16[64,8192]{1,0:T(8,128)(2,1)S(1)}, u32[]{:S(2)}, u32[]{:S(2)}) collective-permute-start(bf16[64,8192]{1,0:T(8,128)(2,1)} %get-tuple-element.26), channel_id=1, source_target_pairs={{0,8},{8,0},{16,24},{24,16},{1,9},{9,1},{17,25},{25,17},{2,10},{10... | collective-permute-start | bytes 3145736 | tf_op jit(solution)/shard_map/ppermute | solution.py:13
  24.8 47.3 %collective-permute-start.1 = (bf16[64,8192]{1,0:T(8,128)(2,1)}, bf16[64,8192]{1,0:T(8,128)(2,1)S(1)}, u32[]{:S(2)}, u32[]{:S(2)}) collective-permute-start(bf16[64,8192]{1,0:T(8,128)(2,1)} %get-tuple-element.28), channel_id=1, source_target_pairs={{0,16},{8,24},{16,0},{24,8},{1,17},{9,25},{17,1},{25,9},{2,18},{10... | collective-permute-start | bytes 3145736 | tf_op jit(solution)/shard_map/ppermute | solution.py:13
  26.4 46.8 %collective-permute-start.2 = (bf16[64,8192]{1,0:T(8,128)(2,1)}, bf16[64,8192]{1,0:T(8,128)(2,1)}, u32[]{:S(2)}, u32[]{:S(2)}) collective-permute-start(bf16[64,8192]{1,0:T(8,128)(2,1)} %get-tuple-element.27), channel_id=1, source_target_pairs={{0,24},{8,16},{16,8},{24,0},{1,25},{9,17},{17,9},{25,1},{2,26},{10... | collective-permute-start | bytes 3145736 | tf_op jit(solution)/shard_map/ppermute | solution.py:13
  27.1 51.9 %copy-start.9 = (bf16[1,64,8192]{2,1,0:T(8,128)(2,1)S(1)}, bf16[1,64,8192]{2,1,0:T(8,128)(2,1)}, u32[]{:S(2)}) copy-start(bf16[1,64,8192]{2,1,0:T(8,128)(2,1)} %param.9) | copy-start | bytes 3145732
  49.0 23.1 %copy-start.7 = (bf16[64,8192]{1,0:T(8,128)(2,1)}, bf16[64,8192]{1,0:T(8,128)(2,1)S(1)}, u32[]{:S(2)}) copy-start(bf16[64,8192]{1,0:T(8,128)(2,1)S(1)} %collective-permute-done) | copy-start | bytes 3145732
  72.2 1.0 copy-start.8
  79.0 1.3 copy-start.2
  80.3 31.4 %copy-start.6 = (bf16[64,8192]{1,0:T(8,128)(2,1)}, bf16[64,8192]{1,0:T(8,128)(2,1)S(1)}, u32[]{:S(2)}) copy-start(bf16[64,8192]{1,0:T(8,128)(2,1)S(1)} %fusion.7) | copy-start | bytes 3145732
  113.2 162.0 %all-gather.5.cloned.1.call-start = ((), (), s32[]{:S(2)}) async-start(), calls=%async_computation.2 | async-start | bytes 4718592 | tf_op jit(solution)/shard_map/all_gather | solution.py:33
  114.0 39.5 %collective-permute-start.4 = (bf16[64,8192]{1,0:T(8,128)(2,1)}, bf16[64,8192]{1,0:T(8,128)(2,1)}, u32[]{:S(2)}, u32[]{:S(2)}) collective-permute-start(bf16[64,8192]{1,0:T(8,128)(2,1)} %get-tuple-element.24), channel_id=1, source_target_pairs={{8,0},{16,8},{24,16},{9,1},{17,9},{25,17},{10,2},{18,10},{26,18},{... | collective-permute-start | bytes 3145736 | tf_op jit(solution)/shard_map/ppermute | solution.py:23
  115.3 60.7 %collective-permute-start.5 = (bf16[64,8192]{1,0:T(8,128)(2,1)}, bf16[64,8192]{1,0:T(8,128)(2,1)}, u32[]{:S(2)}, u32[]{:S(2)}) collective-permute-start(bf16[64,8192]{1,0:T(8,128)(2,1)} %get-tuple-element.20), channel_id=1, source_target_pairs={{8,0},{16,8},{24,16},{9,1},{17,9},{25,17},{10,2},{18,10},{26,18},{... | collective-permute-start | bytes 3145736 | tf_op jit(solution)/shard_map/ppermute | solution.py:23
  116.8 80.1 %collective-permute-start.3 = (bf16[64,8192]{1,0:T(8,128)(2,1)}, bf16[64,8192]{1,0:T(8,128)(2,1)}, u32[]{:S(2)}, u32[]{:S(2)}) collective-permute-start(bf16[64,8192]{1,0:T(8,128)(2,1)} %copy-done.6), channel_id=1, source_target_pairs={{8,0},{16,8},{24,16},{9,1},{17,9},{25,17},{10,2},{18,10},{26,18},{... | collective-permute-start | bytes 3145736 | tf_op jit(solution)/shard_map/ppermute | solution.py:23
  154.9 22.5 %copy-start.3 = (f32[64,8192]{1,0:T(8,128)S(1)}, f32[64,8192]{1,0:T(8,128)}, u32[]{:S(2)}) copy-start(f32[64,8192]{1,0:T(8,128)} %copy-done.2) | copy-start | bytes 6291460
  181.3 6.7 %copy-start.5 = (f32[86,8192]{1,0:T(8,128)S(1)}, f32[86,8192]{1,0:T(8,128)}, u32[]{:S(2)}) copy-start(f32[86,8192]{1,0:T(8,128)} %get-tuple-element.29) | copy-start | bytes 8454148
  275.2 10.9 %copy-start.1 = (bf16[1024,256]{1,0:T(8,128)(2,1)S(1)}, bf16[1024,256]{1,0:T(8,128)(2,1)}, u32[]{:S(2)}) copy-start(bf16[1024,256]{1,0:T(8,128)(2,1)} %param.7) | copy-start | bytes 1572868
Sparse Core Ops, SparseCore 0:
  113.3 112.3 all-gather.2
  227.4 47.7 all-gather.4
where the time goes:
time: 293 us
  waiting for transfers between devices  175 us (60%)
  blocking collectives  31.3 us (11%)
  local copies, waits for them, and re-layouts  27.4 us (9%)
  matrix products  19 us (6%)
  other arithmetic  17 us (6%)
  between operations  14.9 us (5%)
  starting transfers between devices  8.58 us (3%)
    ppermute x3, waiting for transfers between devices, to_front(): return lax.ppermute(block, axis, [(i, i - 1) for i in range(1, n)])  60.5 us
    ppermute x3, waiting for transfers between devices, exchange(): return lax.ppermute(block, axis, [(i, partner(i, k, n)) for i in range(n)])  45 us
    all_gather x1, waiting for transfers between devices, body(): input_all = lax.all_gather(next_input, 'mp', axis=1, tiled=True)  42.9 us
    all_to_all x1, blocking collectives, body(): lax.all_to_all(new_weight, 'mp', split_axis=1, concat_axis=0, tiled=True)  31.3 us
    all_gather x1, waiting for transfers between devices, body(): weight_cols = lax.all_gather(weight_part, 'dp', axis=1, tiled=True)  25.5 us
    broadcast_in_dim x2, local copies, waits for them, and re-layouts, mine(): return lax.dynamic_slice_in_dim(rows, begin, shard_rows, 0)[None]  11.4 us
    dot_general x1, matrix products, body(): lax.dot_general(activations, out_grad, (((0,), (0,)), ((), ())), preferre...  10.7 us
    convert_element_type x3, other arithmetic, mine(): behind = to_front(block.astype(jnp.bfloat16), 'dp').astype(block.dtype)  8.57 us
  transfers between devices with their start and end apart: 8, of which 7 were waited for; matrix products, arithmetic and copies ran while one was open for 10% of the time, Pallas kernels for 0%

commit v1 on v0

--- a/solution.py
+++ b/solution.py
@@ -30,7 +30,12 @@
     width = old_weight.shape[2]
     held_rows = old_rows * owners
     shard_rows = (held_rows + owners - 2) // (owners - 1)
-    input_all = lax.all_gather(next_input, "mp", axis=1, tiled=True)
+    ring = [next_input]
+    for hop in range(7):
+        ring.append(lax.ppermute(ring[-1], "mp", [(dev, (dev + 1) % 8) for dev in range(8)]))
+    input_all = jnp.roll(
+        jnp.concatenate(ring[::-1], axis=1), (lax.axis_index("mp") + 1) * ring[0].shape[1], axis=1
+    )
     part = lax.dot_general(
         activations, out_grad, (((0,), (0,)), ((), ())), preferred_element_type=jnp.float32
     ).astype(jnp.bfloat16)

time: 293 us -> 258 us (0.88); the launches traced: 293 us -> 254 us
  waiting for transfers between devices: 175 us -> 140 us
  blocking collectives: 31.3 us -> 0 us
  local copies, waits for them, and re-layouts: 27.4 us -> 50.7 us
  starting transfers between devices: 8.58 us -> 13.9 us
    ppermute x0 -> x7, waiting for transfers between devices: none -> 52.1 us  [body(): lax.ppermute(ring[-1], 'mp', [(dev, (dev + 1) % 8) for dev in range(8)])]
    all_gather x1 -> x0, waiting for transfers between devices: 42.9 us -> none  [body(): input_all = lax.all_gather(next_input, 'mp', axis=1, tiled=True)]
    all_to_all x1 -> x0, blocking collectives: 31.3 us -> none  [body(): lax.all_to_all(new_weight, 'mp', split_axis=1, concat_axis=0, tiled=True)]
    all_gather x1, waiting for transfers between devices: 25.5 us -> 0.01 us  [body(): weight_cols = lax.all_gather(weight_part, 'dp', axis=1, tiled=True)]
    unnamed x21 -> x51, local copies, waits for them, and re-layouts: 5.95 us -> 28.3 us
    ppermute x3, waiting for transfers between devices: 60.5 us -> 42.2 us  [to_front(): return lax.ppermute(block, axis, [(i, i - 1) for i in range(1, n)])]
    all_to_all x0 -> x1, starting transfers between devices: none -> 4.88 us  [body(): lax.all_to_all(new_weight, 'mp', split_axis=1, concat_axis=0, tiled=True)]
  transfers between devices with their start and end apart: 8 -> 15, of which waited for: 7 -> 10; matrix products, arithmetic and copies ran while one was open for 10% -> 21% of each run, Pallas kernels for 0% -> 0%
where the time goes in v1:
time: 258 us; the launch traced here: 254 us
  waiting for transfers between devices  140 us (54%)
  local copies, waits for them, and re-layouts  50.7 us (20%)
  matrix products  18.7 us (7%)
  other arithmetic  15.6 us (6%)
  between operations  15 us (6%)
  starting transfers between devices  13.9 us (5%)
    ppermute x7, waiting for transfers between devices, body(): lax.ppermute(ring[-1], 'mp', [(dev, (dev + 1) % 8) for dev in range(8)])  52.1 us
    ppermute x3, waiting for transfers between devices, exchange(): return lax.ppermute(block, axis, [(i, partner(i, k, n)) for i in range(n)])  45.4 us
    ppermute x3, waiting for transfers between devices, to_front(): return lax.ppermute(block, axis, [(i, i - 1) for i in range(1, n)])  42.2 us
    unnamed x51, local copies, waits for them, and re-layouts  28.3 us
    broadcast_in_dim x2, local copies, waits for them, and re-layouts, mine(): return lax.dynamic_slice_in_dim(rows, begin, shard_rows, 0)[None]  11.3 us
    dot_general x1, matrix products, body(): lax.dot_general(activations, out_grad, (((0,), (0,)), ((), ())), preferre...  10.7 us
    convert_element_type x3, other arithmetic, mine(): behind = to_front(block.astype(jnp.bfloat16), 'dp').astype(block.dtype)  8.57 us
    dot_general x1, matrix products, body(): jnp.dot(input_all, weight_cols, preferred_element_type=jnp.float32)  7.91 us
  transfers between devices with their start and end apart: 15, of which 10 were waited for; matrix products, arithmetic and copies ran while one was open for 21% of the time, Pallas kernels for 0%

profile of v1, /device:TPU:0, one launch (start us, length us, event | category | flops | bytes accessed | tf_op | source)
XLA Modules:
  0.0 253.7 jit_solution(16480160155095478219)
XLA Ops:
  7.2 1.0 copy-done
  8.2 10.7 %convolution_convert_fusion = bf16[256,8192]{1,0:T(8,128)(2,1)S(1)} fusion(bf16[1024,256]{1,0:T(8,128)(2,1)S(1)} %copy-done, bf16[1024,8192]{1,0:T(8,128)(2,1)} %param.8), kind=kOutput, calls=%fused_computation | convolution fusion | flops 4297064448 | bytes 21495808 | tf_op jit(solution)/shard_map/dot_general | solution.py:39
  19.0 1.9 copy-done.4
  20.9 1.7 dynamic-slice_bitcast_fusion.2
  22.7 2.9 %collective-permute-start = (bf16[64,8192]{1,0:T(8,128)(2,1)}, bf16[64,8192]{1,0:T(8,128)(2,1)S(1)}, u32[]{:S(2)}, u32[]{:S(2)}) collective-permute-start(bf16[64,8192]{1,0:T(8,128)(2,1)} %get-tuple-element.10), channel_id=1, source_target_pairs={{0,8},{8,0},{16,24},{24,16},{1,9},{9,1},{17,25},{25,17},{2,10},{10... | collective-permute-start | bytes 3145736 | tf_op jit(solution)/shard_map/ppermute | solution.py:13
  25.6 1.5 collective-permute-start.2
  27.9 21.9 %collective-permute-done = bf16[64,8192]{1,0:T(8,128)(2,1)S(1)} collective-permute-done((bf16[64,8192]{1,0:T(8,128)(2,1)}, bf16[64,8192]{1,0:T(8,128)(2,1)S(1)}, u32[]{:S(2)}, u32[]{:S(2)}) %collective-permute-start) | collective-permute-done | bytes 1048608 | tf_op jit(solution)/shard_map/ppermute | solution.py:13
  49.8 23.0 %collective-permute-done.2 = bf16[64,8192]{1,0:T(8,128)(2,1)S(1)} collective-permute-done((bf16[64,8192]{1,0:T(8,128)(2,1)}, bf16[64,8192]{1,0:T(8,128)(2,1)S(1)}, u32[]{:S(2)}, u32[]{:S(2)}) %collective-permute-start.2) | collective-permute-done | bytes 1048608 | tf_op jit(solution)/shard_map/ppermute | solution.py:13
  72.8 1.0 copy-done.16
  74.2 5.9 %fusion.17 = (bf16[64,8192]{1,0:T(8,128)(2,1)}, f32[64,8192]{1,0:T(8,128)S(1)}, bf16[64,8192]{1,0:T(8,128)(2,1)}, f32[64,8192]{1,0:T(8,128)S(1)}) fusion(bf16[64,8192]{1,0:T(8,128)(2,1)} %copy-done.16, bf16[64,8192]{1,0:T(8,128)(2,1)} %collective-permute-done.1, bf16[64,8192]{1,0:T(8,128)(2,1)} %copy-done.15, bf16[4,64,8192]{2,1,0:T(8,128)(2,1)} %bitcast.39, ...), kind=kLoop, calls=%fused_computation.48 | loop fusion | flops 8388608 | bytes 14680068 | tf_op jit(solution)/shard_map/convert_element_type | solution.py:62
  80.1 1.1 fusion.9
  81.2 1.0 copy-done.6
  82.1 1.1 copy.17
  83.2 4.9 %all-to-all-start = ((bf16[64,8,1024]{2,0,1:T(8,128)(2,1)}), bf16[64,8,1024]{2,0,1:T(8,128)(2,1)}, u32[]{:S(2)}, u32[]{:S(2)}) async-start(bf16[64,8,1024]{2,0,1:T(8,128)(2,1)} %bitcast.42), calls=%async_computation | async-start | bytes 2097152 | tf_op jit(solution)/shard_map/all_to_all | solution.py:54
  88.7 27.1 %collective-permute-done.7 = bf16[1024,256]{1,0:T(8,128)(2,1)S(1)} collective-permute-done((bf16[1024,256]{1,0:T(8,128)(2,1)S(1)}, bf16[1024,256]{1,0:T(8,128)(2,1)S(1)}, u32[]{:S(2)}, u32[]{:S(2)}) %collective-permute-start.7) | collective-permute-done | bytes 524320 | tf_op jit(solution)/shard_map/ppermute | solution.py:35
  116.5 1.3 collective-permute-start.5
  117.8 1.3 collective-permute-start.4
  119.1 7.8 %collective-permute-done.8 = bf16[1024,256]{1,0:T(8,128)(2,1)S(1)} collective-permute-done((bf16[1024,256]{1,0:T(8,128)(2,1)S(1)}, bf16[1024,256]{1,0:T(8,128)(2,1)S(1)}, u32[]{:S(2)}, u32[]{:S(2)}) %collective-permute-start.8) | collective-permute-done | bytes 524320 | tf_op jit(solution)/shard_map/ppermute | solution.py:35
  127.7 10.5 %collective-permute-done.9 = bf16[1024,256]{1,0:T(8,128)(2,1)} collective-permute-done((bf16[1024,256]{1,0:T(8,128)(2,1)S(1)}, bf16[1024,256]{1,0:T(8,128)(2,1)}, u32[]{:S(2)}, u32[]{:S(2)}) %collective-permute-start.9) | collective-permute-done | bytes 524320 | tf_op jit(solution)/shard_map/ppermute | solution.py:35
  138.2 2.8 %copy.13 = bf16[8,64,1024]{2,0,1:T(8,128)(2,1)} copy(bf16[8,64,1024]{2,1,0:T(8,128)(2,1)} %bitcast.11) | data formatting | bytes 2097152 | tf_op jit(solution)/shard_map/all_to_all | solution.py:54
  141.3 1.4 collective-permute-start.3
  142.7 2.2 collective-permute-done.5
  144.8 1.4 convert_element_type.59
  146.2 32.3 %collective-permute-done.4 = bf16[64,8192]{1,0:T(8,128)(2,1)} collective-permute-done((bf16[64,8192]{1,0:T(8,128)(2,1)}, bf16[64,8192]{1,0:T(8,128)(2,1)}, u32[]{:S(2)}, u32[]{:S(2)}) %collective-permute-start.4) | collective-permute-done | bytes 1048608 | tf_op jit(solution)/shard_map/ppermute | solution.py:23
  178.5 1.4 convert_element_type.57
  180.0 3.9 %fusion.3 = (f32[86,8192]{1,0:T(8,128)}, f32[86,8192]{1,0:T(8,128)}) fusion(s32[]{:T(128)S(6)} %select_n.35, f32[64,8192]{1,0:T(8,128)S(1)} %get-tuple-element.5, f32[64,8192]{1,0:T(8,128)S(1)} %convert_element_type.59, f32[86]{0:T(128)S(1)} %pad_dynamic-slice_fusion.6, f32[64,8192]{1,0:T(8,128)S(1)} %convert_element_type.57, f32[64,8192]{1,0:T(8,128)S(1)} %copy-done.3), kind=kLoop, calls=%fused_computation.11 | loop fusion | flops 2818048 | bytes 14025052 | tf_op jit(solution)/shard_map/concatenate | solution.py:63
  183.9 6.8 %collective-permute-done.11 = bf16[1024,256]{1,0:T(8,128)(2,1)} collective-permute-done((bf16[1024,256]{1,0:T(8,128)(2,1)}, bf16[1024,256]{1,0:T(8,128)(2,1)}, u32[]{:S(2)}, u32[]{:S(2)}) %collective-permute-start.11) | collective-permute-done | bytes 524320 | tf_op jit(solution)/shard_map/ppermute | solution.py:35
  190.7 7.7 %collective-permute-done.3 = bf16[64,8192]{1,0:T(8,128)(2,1)S(1)} collective-permute-done((bf16[64,8192]{1,0:T(8,128)(2,1)}, bf16[64,8192]{1,0:T(8,128)(2,1)S(1)}, u32[]{:S(2)}, u32[]{:S(2)}) %collective-permute-start.3) | collective-permute-done | bytes 1048608 | tf_op jit(solution)/shard_map/ppermute | solution.py:23
  198.5 2.0 fusion.15
  200.5 6.5 %broadcast_in_dim.15 = f32[1,86,8192]{2,0,1:T(1,128)} reshape(f32[86,8192]{1,0:T(8,128)} %get-tuple-element.13) | data formatting | bytes 5636096 | tf_op jit(solution)/shard_map/broadcast_in_dim | solution.py:64
  207.0 4.7 %broadcast_in_dim.14 = f32[1,86,8192]{2,0,1:T(1,128)} reshape(f32[86,8192]{1,0:T(8,128)S(1)} %copy-done.5) | data formatting | bytes 5636096 | tf_op jit(solution)/shard_map/broadcast_in_dim | solution.py:64
  211.8 2.1 constant_dynamic-update-slice_fusion.15
  213.8 1.9 constant_dynamic-update-slice_fusion.14
  215.8 2.0 constant_dynamic-update-slice_fusion.13
  217.7 1.9 constant_dynamic-update-slice_fusion.12
  219.7 0.9 constant_dynamic-update-slice_fusion.11
  220.6 0.9 constant_dynamic-update-slice_fusion.10
  221.4 0.9 constant_dynamic-update-slice_fusion.9
  222.3 0.9 constant_dynamic-update-slice_fusion.8
  223.2 1.9 constant_dynamic-update-slice_fusion.7
  225.1 1.9 constant_dynamic-update-slice_fusion.6
  227.1 1.9 constant_dynamic-update-slice_fusion.5
  229.0 1.9 constant_dynamic-update-slice_fusion.4
  230.9 0.9 constant_dynamic-update-slice_fusion.3
  231.8 0.9 constant_dynamic-update-slice_fusion.2
  233.6 0.9 constant_dynamic-update-slice_fusion
  234.4 4.5 %copy.14 = bf16[8,256,1024]{2,1,0:T(8,128)(2,1)S(1)} copy(bf16[8,256,1024]{2,0,1:T(8,128)(2,1)} %all-gather.2.cloned.1.call-done) | data formatting | bytes 8388608 | tf_op jit(solution)/shard_map/all_gather | solution.py:57
  239.0 7.9 %fusion.10 = bf16[1024,1024]{1,0:T(8,128)(2,1)} fusion(bf16[2048,1024]{1,0:T(8,128)(2,1)S(1)} %bitcast.41, bf16[1024,4096]{1,0:T(8,128)(2,1)} %constant_dynamic-update-slice_fusion, s32[]{:T(128)S(6)} %select_n.37), kind=kOutput, calls=%fused_computation.21 | convolution fusion | flops 4296015872 | bytes 10485764 | tf_op jit(solution)/shard_map/dot_general | solution.py:67
  (53 shorter events, 3.9 us)
Async XLA Ops:
  7.2 1.1 copy-start
  19.0 2.0 copy-start.4
  19.0 8.2 %copy-start.8 = (bf16[1024,256]{1,0:T(8,128)(2,1)S(1)}, bf16[1024,256]{1,0:T(8,128)(2,1)}, u32[]{:S(2)}) copy-start(bf16[1024,256]{1,0:T(8,128)(2,1)} %param.13) | copy-start | bytes 1572868
  22.7 27.1 %collective-permute-start = (bf16[64,8192]{1,0:T(8,128)(2,1)}, bf16[64,8192]{1,0:T(8,128)(2,1)S(1)}, u32[]{:S(2)}, u32[]{:S(2)}) collective-permute-start(bf16[64,8192]{1,0:T(8,128)(2,1)} %get-tuple-element.10), channel_id=1, source_target_pairs={{0,8},{8,0},{16,24},{24,16},{1,9},{9,1},{17,25},{25,17},{2,10},{10... | collective-permute-start | bytes 3145736 | tf_op jit(solution)/shard_map/ppermute | solution.py:13
  25.6 47.1 %collective-permute-start.2 = (bf16[64,8192]{1,0:T(8,128)(2,1)}, bf16[64,8192]{1,0:T(8,128)(2,1)S(1)}, u32[]{:S(2)}, u32[]{:S(2)}) collective-permute-start(bf16[64,8192]{1,0:T(8,128)(2,1)} %get-tuple-element.11), channel_id=1, source_target_pairs={{0,24},{8,16},{16,8},{24,0},{1,25},{9,17},{17,9},{25,1},{2,26},{10... | collective-permute-start | bytes 3145736 | tf_op jit(solution)/shard_map/ppermute | solution.py:13
  27.1 47.1 %collective-permute-start.1 = (bf16[64,8192]{1,0:T(8,128)(2,1)}, bf16[64,8192]{1,0:T(8,128)(2,1)}, u32[]{:S(2)}, u32[]{:S(2)}) collective-permute-start(bf16[64,8192]{1,0:T(8,128)(2,1)} %get-tuple-element.12), channel_id=1, source_target_pairs={{0,16},{8,24},{16,0},{24,8},{1,17},{9,25},{17,1},{25,9},{2,18},{10... | collective-permute-start | bytes 3145736 | tf_op jit(solution)/shard_map/ppermute | solution.py:13
  27.1 61.0 %collective-permute-start.6 = (bf16[1024,256]{1,0:T(8,128)(2,1)S(1)}, bf16[1024,256]{1,0:T(8,128)(2,1)S(1)}, u32[]{:S(2)}, u32[]{:S(2)}) collective-permute-start(bf16[1024,256]{1,0:T(8,128)(2,1)S(1)} %copy-done.8), channel_id=1, source_target_pairs={{0,1},{1,2},{2,3},{3,4},{4,5},{5,6},{6,7},{7,0},{8,9},{9,10},{10,1... | collective-permute-start | bytes 1572872 | tf_op jit(solution)/shard_map/ppermute | solution.py:35
  27.9 52.2 %copy-start.17 = (bf16[1,64,8192]{2,1,0:T(8,128)(2,1)S(1)}, bf16[1,64,8192]{2,1,0:T(8,128)(2,1)}, u32[]{:S(2)}) copy-start(bf16[1,64,8192]{2,1,0:T(8,128)(2,1)} %param.9) | copy-start | bytes 3145732
  49.8 23.0 %copy-start.15 = (bf16[64,8192]{1,0:T(8,128)(2,1)}, bf16[64,8192]{1,0:T(8,128)(2,1)S(1)}, u32[]{:S(2)}) copy-start(bf16[64,8192]{1,0:T(8,128)(2,1)S(1)} %collective-permute-done) | copy-start | bytes 3145732
  72.8 1.0 copy-start.16
  80.1 3.1 %copy-start.2 = (f32[64,8192]{1,0:T(8,128)}, f32[64,8192]{1,0:T(8,128)S(1)}, u32[]{:S(2)}) copy-start(f32[64,8192]{1,0:T(8,128)S(1)} %get-tuple-element.9) | copy-start | bytes 6291460
  81.2 1.0 copy-start.6
  83.2 55.0 %all-to-all-start = ((bf16[64,8,1024]{2,0,1:T(8,128)(2,1)}), bf16[64,8,1024]{2,0,1:T(8,128)(2,1)}, u32[]{:S(2)}, u32[]{:S(2)}) async-start(bf16[64,8,1024]{2,0,1:T(8,128)(2,1)} %bitcast.42), calls=%async_computation | async-start | bytes 2097152 | tf_op jit(solution)/shard_map/all_to_all | solution.py:54
  88.1 146.3 %all-gather.2.cloned.1.call-start = ((), (), s32[]{:S(2)}) async-start(), calls=%async_computation.1 | async-start | bytes 5242880 | tf_op jit(solution)/shard_map/all_gather | solution.py:57
  88.1 91.8 %copy-start.9 = (bf16[1024,256]{1,0:T(8,128)(2,1)}, bf16[1024,256]{1,0:T(8,128)(2,1)S(1)}, u32[]{:S(2)}) copy-start(bf16[1024,256]{1,0:T(8,128)(2,1)S(1)} %collective-permute-done.6) | copy-start | bytes 1572868
  88.2 27.6 %collective-permute-start.7 = (bf16[1024,256]{1,0:T(8,128)(2,1)S(1)}, bf16[1024,256]{1,0:T(8,128)(2,1)S(1)}, u32[]{:S(2)}, u32[]{:S(2)}) collective-permute-start(bf16[1024,256]{1,0:T(8,128)(2,1)S(1)} %collective-permute-done.6), channel_id=1, source_target_pairs={{0,1},{1,2},{2,3},{3,4},{4,5},{5,6},{6,7},{7,0},{8,9},{9,10},{10,1... | collective-permute-start | bytes 1572872 | tf_op jit(solution)/shard_map/ppermute | solution.py:35
  115.7 0.8 copy-start.11
  116.5 10.4 %collective-permute-start.8 = (bf16[1024,256]{1,0:T(8,128)(2,1)S(1)}, bf16[1024,256]{1,0:T(8,128)(2,1)S(1)}, u32[]{:S(2)}, u32[]{:S(2)}) collective-permute-start(bf16[1024,256]{1,0:T(8,128)(2,1)S(1)} %collective-permute-done.7), channel_id=1, source_target_pairs={{0,1},{1,2},{2,3},{3,4},{4,5},{5,6},{6,7},{7,0},{8,9},{9,10},{10,1... | collective-permute-start | bytes 1572872 | tf_op jit(solution)/shard_map/ppermute | solution.py:35
  116.5 28.3 %collective-permute-start.5 = (bf16[64,8192]{1,0:T(8,128)(2,1)}, bf16[64,8192]{1,0:T(8,128)(2,1)}, u32[]{:S(2)}, u32[]{:S(2)}) collective-permute-start(bf16[64,8192]{1,0:T(8,128)(2,1)} %get-tuple-element.4), channel_id=1, source_target_pairs={{8,0},{16,8},{24,16},{9,1},{17,9},{25,17},{10,2},{18,10},{26,18},{... | collective-permute-start | bytes 3145736 | tf_op jit(solution)/shard_map/ppermute | solution.py:23
  117.8 60.7 %collective-permute-start.4 = (bf16[64,8192]{1,0:T(8,128)(2,1)}, bf16[64,8192]{1,0:T(8,128)(2,1)}, u32[]{:S(2)}, u32[]{:S(2)}) collective-permute-start(bf16[64,8192]{1,0:T(8,128)(2,1)} %get-tuple-element.8), channel_id=1, source_target_pairs={{8,0},{16,8},{24,16},{9,1},{17,9},{25,17},{10,2},{18,10},{26,18},{... | collective-permute-start | bytes 3145736 | tf_op jit(solution)/shard_map/ppermute | solution.py:23
  126.9 0.8 copy-start.13
  127.7 10.5 %collective-permute-start.9 = (bf16[1024,256]{1,0:T(8,128)(2,1)S(1)}, bf16[1024,256]{1,0:T(8,128)(2,1)}, u32[]{:S(2)}, u32[]{:S(2)}) collective-permute-start(bf16[1024,256]{1,0:T(8,128)(2,1)S(1)} %collective-permute-done.8), channel_id=1, source_target_pairs={{0,1},{1,2},{2,3},{3,4},{4,5},{5,6},{6,7},{7,0},{8,9},{9,10},{10,1... | collective-permute-start | bytes 1572872 | tf_op jit(solution)/shard_map/ppermute | solution.py:35
  138.2 41.7 %collective-permute-start.10 = (bf16[1024,256]{1,0:T(8,128)(2,1)}, bf16[1024,256]{1,0:T(8,128)(2,1)}, u32[]{:S(2)}, u32[]{:S(2)}) collective-permute-start(bf16[1024,256]{1,0:T(8,128)(2,1)} %collective-permute-done.9), channel_id=1, source_target_pairs={{0,1},{1,2},{2,3},{3,4},{4,5},{5,6},{6,7},{7,0},{8,9},{9,10},{10,1... | collective-permute-start | bytes 1572872 | tf_op jit(solution)/shard_map/ppermute | solution.py:35
  141.1 38.9 %copy-start.3 = (f32[64,8192]{1,0:T(8,128)S(1)}, f32[64,8192]{1,0:T(8,128)}, u32[]{:S(2)}) copy-start(f32[64,8192]{1,0:T(8,128)} %copy-done.2) | copy-start | bytes 6291460
  141.3 57.2 %collective-permute-start.3 = (bf16[64,8192]{1,0:T(8,128)(2,1)}, bf16[64,8192]{1,0:T(8,128)(2,1)S(1)}, u32[]{:S(2)}, u32[]{:S(2)}) collective-permute-start(bf16[64,8192]{1,0:T(8,128)(2,1)} %copy-done.6), channel_id=1, source_target_pairs={{8,0},{16,8},{24,16},{9,1},{17,9},{25,17},{10,2},{18,10},{26,18},{... | collective-permute-start | bytes 3145736 | tf_op jit(solution)/shard_map/ppermute | solution.py:23
  179.9 18.5 %copy-start.7 = (bf16[64,8192]{1,0:T(8,128)(2,1)S(1)}, bf16[64,8192]{1,0:T(8,128)(2,1)}, u32[]{:S(2)}) copy-start(bf16[64,8192]{1,0:T(8,128)(2,1)} %copy-done.6) | copy-start | bytes 3145732
  179.9 10.8 %collective-permute-start.11 = (bf16[1024,256]{1,0:T(8,128)(2,1)}, bf16[1024,256]{1,0:T(8,128)(2,1)}, u32[]{:S(2)}, u32[]{:S(2)}) collective-permute-start(bf16[1024,256]{1,0:T(8,128)(2,1)} %collective-permute-done.10), channel_id=1, source_target_pairs={{0,1},{1,2},{2,3},{3,4},{4,5},{5,6},{6,7},{7,0},{8,9},{9,10},{10,1... | collective-permute-start | bytes 1572872 | tf_op jit(solution)/shard_map/ppermute | solution.py:35
  183.9 23.1 %copy-start.5 = (f32[86,8192]{1,0:T(8,128)S(1)}, f32[86,8192]{1,0:T(8,128)}, u32[]{:S(2)}) copy-start(f32[86,8192]{1,0:T(8,128)} %get-tuple-element.14) | copy-start | bytes 8454148
  190.7 21.1 %collective-permute-start.12 = (bf16[1024,256]{1,0:T(8,128)(2,1)}, bf16[1024,256]{1,0:T(8,128)(2,1)}, u32[]{:S(2)}, u32[]{:S(2)}) collective-permute-start(bf16[1024,256]{1,0:T(8,128)(2,1)} %collective-permute-done.11), channel_id=1, source_target_pairs={{0,1},{1,2},{2,3},{3,4},{4,5},{5,6},{6,7},{7,0},{8,9},{9,10},{10,1... | collective-permute-start | bytes 1572872 | tf_op jit(solution)/shard_map/ppermute | solution.py:35
  211.8 7.9 %copy-start.14 = (bf16[1024,256]{1,0:T(8,128)(2,1)S(1)}, bf16[1024,256]{1,0:T(8,128)(2,1)}, u32[]{:S(2)}) copy-start(bf16[1024,256]{1,0:T(8,128)(2,1)} %copy-done.13) | copy-start | bytes 1572868
  211.8 8.8 %copy-start.12 = (bf16[1024,256]{1,0:T(8,128)(2,1)S(1)}, bf16[1024,256]{1,0:T(8,128)(2,1)}, u32[]{:S(2)}) copy-start(bf16[1024,256]{1,0:T(8,128)(2,1)} %copy-done.11) | copy-start | bytes 1572868
  211.8 9.6 %copy-start.10 = (bf16[1024,256]{1,0:T(8,128)(2,1)S(1)}, bf16[1024,256]{1,0:T(8,128)(2,1)}, u32[]{:S(2)}) copy-start(bf16[1024,256]{1,0:T(8,128)(2,1)} %copy-done.9) | copy-start | bytes 1572868
  238.9 7.9 %copy-start.1 = (bf16[1024,256]{1,0:T(8,128)(2,1)S(1)}, bf16[1024,256]{1,0:T(8,128)(2,1)}, u32[]{:S(2)}) copy-start(bf16[1024,256]{1,0:T(8,128)(2,1)} %param.7) | copy-start | bytes 1572868
Sparse Core Ops, SparseCore 0:
  141.2 91.0 all-gather.1
